TPU v7x, 256 devices: a whole 4x4x8 slice. The times are simulated.
256 devices in a mesh: band: 8 (over x, y_lo), fft: 32 (over z, y_hi, core).
Axes of the slice: x: 4, y: 4 (y_hi: 2, y_lo: 2; y = y_hi * 2 + y_lo), z: 8, core: 2. Of those that a mesh axis runs over, the one named last changes fastest.
Arguments:
- orbitals: float32 [8, 256, 256, 256], P('band', 'fft'), may hold values from -6 to 6
- band_ids: int32 [8], replicated, may hold values from 0 to 7, each once
- owners: int32 [2], replicated, may hold values from 0 to 7, as said below
Outputs:
- exchange_potential: float32 [8, 256, 256, 256], P('band', 'fft')
Inputs may be any that keep to these rules, and one draw needn't show every extreme that they name: `band_ids`: each band number stands in exactly one slot; slot s belongs to band group s. `owners`: 2 different band numbers, one of which is 7.
All inputs are finite; a program needn't handle non-finite values.
Results may differ from a plain program's by a relative error of at most 0.0003.
Values sent between devices are 32-bit elements; how exact they have to be, the bound alone decides.
A program may use at most 64 MiB of HBM per device.

v0:
```python
import math

import jax
import jax.numpy as jnp
import ml_dtypes
import numpy as np
from jax import lax
from jax.experimental import pallas as pl
from jax.experimental.pallas import tpu as pltpu
from jax.sharding import PartitionSpec as P

MESH = pl.DeviceIdType.MESH
F32 = jnp.float32
BF16 = jnp.bfloat16
cell_length = 46.9

POINTS = 256
FREQS = 128
PLANES = 8
CHIPS = 16
VMEM_MIB = 60
ROWS = ((0, 88), (88, 88), (176, 80))
ORDER = (0, 1, 2, 5, 6, 3, 4, 7)
EARLY = 5
TREES = (
    ((0, 2, 4, 5), (3,), (2, 4)),
    ((7,), (0, 6, 4, 7, 5), (6,)),
    ((1, 3), (1,), (0, 3, 5, 7)),
)
DEPTHS = ((0, 3, 1, 2, 2, 3, 3, 4), (0, 3, 3, 4, 2, 3, 1, 2), (0, 1, 3, 2, 4, 3, 3, 2))


def split(value):
    high = value.astype(BF16)
    return high, (value - high.astype(F32)).astype(BF16)


def dot(left, right):
    return jnp.dot(left, right, preferred_element_type=F32)


def quarters(value):
    rows, columns = value.shape[0] // 2, value.shape[1] // 2
    small = (value[:rows, columns:] + value[rows:, :columns]) + value[rows:, columns:]
    return value[:rows, :columns] + small


def kernel(
    orb_ref, ids_ref, owners_ref, tall_in, wide_in, tall_x_in, wide_x_in, out_ref,
    tall_ref, wide_ref, tall_x, wide_x, gathered, held, own, ahead, arrived, back, restored, weights, partial, result,
    in_sem, spread_send, spread_recv, tree_send, tree_recv, ahead_send, ahead_recv, back_send, back_recv, out_sem,
):
    band = lax.axis_index("band")
    place = lax.axis_index("fft")
    my_x, my_y = band // 2, band % 2
    chip, core = place // 2, place % 2

    def band_at(x, y):
        return ((my_x + x) % 4) * 2 + (my_y + y) % 2

    def source(relative):
        return band_at(4 - relative // 2, relative % 2)

    neighbours = (band_at(1, 0), band_at(3, 0), band_at(0, 1))

    load = pltpu.make_async_copy(orb_ref.at[0], own, in_sem.at[0])
    load.start()
    tables = (
        pltpu.make_async_copy(tall_in, tall_ref, in_sem.at[1]),
        pltpu.make_async_copy(wide_in, wide_ref, in_sem.at[2]),
        pltpu.make_async_copy(tall_x_in.at[band], tall_x, in_sem.at[3]),
        pltpu.make_async_copy(wide_x_in.at[band], wide_x, in_sem.at[4]),
    )
    for table in tables:
        table.start()
    barrier = pltpu.get_barrier_semaphore()
    for k in range(1, 8):
        pl.semaphore_signal(
            barrier, inc=1, device_id=((band + k) % 8, place), device_id_type=MESH
        )

    def greet(k, _):
        pl.semaphore_signal(
            barrier, inc=1, device_id=(band, (place + k) % 32), device_id_type=MESH
        )
        return 0

    lax.fori_loop(1, 32, greet, 0)

    pl.semaphore_wait(barrier, 38)
    for relative in (4, 5, 2, 6, 3, 7, 1):
        there = source(relative)
        pltpu.make_async_remote_copy(
            src_ref=orb_ref.at[0, there], dst_ref=gathered.at[band],
            send_sem=spread_send.at[0], recv_sem=spread_recv.at[0],
            device_id=(there, place), device_id_type=MESH,
        ).start()

    kx = lax.broadcasted_iota(jnp.int32, (FREQS, FREQS), 0) - FREQS // 2
    kz = lax.broadcasted_iota(jnp.int32, (FREQS, FREQS), 1) - FREQS // 2

    def weigh(row, _):
        ky = chip * 8 + row - FREQS // 2
        square = kx * kx + kz * kz + ky * ky
        inside = (square > 0) & (square < FREQS * FREQS // 4)
        safe = jnp.where(inside, square, 1).astype(F32)
        scale = cell_length**2 / math.pi / float(POINTS) ** 3
        weights[row] = jnp.where(inside, jnp.float32(scale) / safe, jnp.float32(0.0))
        return 0

    lax.fori_loop(0, 8, weigh, 0)

    load.wait()
    for table in tables:
        table.wait()
    gathered[band] = own[band]
    part = gathered.at[pl.ds(0, 7)]
    pltpu.make_async_copy(part, part, spread_recv.at[0]).wait()
    for o in range(2):
        slot = 0
        for s in range(1, 8):
            slot = jnp.where(ids_ref[s] == owners_ref[o], s, slot)
        held[o, band] = gathered[slot]

    def relay(o, depth):
        for i, (first, count) in enumerate(ROWS):
            for relative in range(8):
                if DEPTHS[i][relative] != depth:
                    continue
                origin = source(relative)
                part = held.at[o, origin, pl.ds(first, count)]
                if depth:
                    pltpu.make_async_copy(part, part, tree_recv.at[o, origin, i]).wait()
                for way in range(3):
                    if relative in TREES[i][way]:
                        pltpu.make_async_remote_copy(
                            src_ref=part, dst_ref=part,
                            send_sem=tree_send.at[o], recv_sem=tree_recv.at[o, origin, i],
                            device_id=(neighbours[way], place), device_id_type=MESH,
                        ).start()

    def plane(k):
        return source(sum(jnp.where(k == n, relative, 0) for n, relative in enumerate(ORDER)))

    def forward(o, k):
        p = plane(k)
        density = held[o, p] * own[p]
        level = jnp.sum(density, keepdims=True) * (1.0 / POINTS**2)
        high, low = split(density - level)
        along_z = quarters(dot(jnp.concatenate([high, low], axis=0), tall_ref[...]))
        high, low = split(along_z)
        along_y = quarters(dot(wide_ref[...], jnp.concatenate([high, low], axis=1)))
        along_y = along_y + jnp.where((kx == 0) & (kz == 0), level * float(POINTS**2), 0.0)
        ahead[o, :, k] = along_y.reshape(CHIPS, 8, FREQS)

    def send_ahead(o, first, count):
        def one(k, _):
            there = (chip + k) % CHIPS
            source = ahead.at[o, there, pl.ds(first, count)]
            target = arrived.at[pl.ds(place * PLANES + first, count)]
            here = there * 2 + o == place

            @pl.when(here)
            def _():
                pltpu.make_async_copy(source, target, ahead_recv.at[0]).start()

            @pl.when(jnp.logical_not(here))
            def _():
                pltpu.make_async_remote_copy(
                    src_ref=source, dst_ref=target,
                    send_sem=ahead_send.at[o], recv_sem=ahead_recv.at[0],
                    device_id=(band, there * 2 + o), device_id_type=MESH,
                ).start()

            return 0

        lax.fori_loop(0, CHIPS, one, 0)

    def transform(o, first, last):
        def one(k, _):
            forward(o, k)
            return 0

        lax.fori_loop(first, last, one, 0)
        send_ahead(o, first, last - first)

    half = PLANES // 2

    def middle(o):
        @pl.when(core == o)
        def _():
            pltpu.make_async_copy(arrived, arrived, ahead_recv.at[0]).wait()

            def one(row, _):
                column = arrived[:, pl.ds(row, 1), :].reshape(POINTS, FREQS)
                level = jnp.sum(column, axis=0, keepdims=True) * (1.0 / POINTS)
                high, low = split(column - level)
                along_x = quarters(dot(wide_x[...], jnp.concatenate([high, low], axis=1)))
                along_x = along_x + jnp.where(kx == 0, level * float(POINTS), 0.0)
                high, low = split(along_x * weights[row])
                pair = jnp.concatenate([high, low], axis=1)
                both = dot(tall_x[...], jnp.concatenate([pair, pair], axis=0))
                back[:, pl.ds(row, 1), :] = (both[:, :FREQS] + both[:, FREQS:]).reshape(POINTS, 1, FREQS)
                return 0

            lax.fori_loop(0, 8, one, 0, unroll=True)
            for h in range(2):
                def one(k, _):
                    there = (place + k) % 32
                    source = back.at[pl.ds(there * PLANES + h * half, half)]
                    target = restored.at[o, chip, pl.ds(h * half, half)]

                    @pl.when(k == 0)
                    def _():
                        pltpu.make_async_copy(source, target, back_recv.at[o, h]).start()

                    @pl.when(k != 0)
                    def _():
                        pltpu.make_async_remote_copy(
                            src_ref=source, dst_ref=target,
                            send_sem=back_send.at[0], recv_sem=back_recv.at[o, h],
                            device_id=(band, there), device_id_type=MESH,
                        ).start()

                    return 0

                lax.fori_loop(0, 32, one, 0)

    def backward(o, k):
        high, low = split(restored[o, :, k].reshape(FREQS, FREQS))
        pair = jnp.concatenate([high, low], axis=1)
        both = dot(tall_ref[...], jnp.concatenate([pair, pair], axis=0))
        high, low = split(both[:, :FREQS] + both[:, FREQS:])
        field = dot(jnp.concatenate([high, low], axis=1), jnp.concatenate([wide_ref[:FREQS], wide_ref[:FREQS]], axis=0))
        field = field + dot(high, wide_ref[FREQS:])
        return held[o, plane(k)] * field
        return held[o, plane(k)]

    relay(0, 0)
    relay(1, 0)
    relay(0, 1)
    relay(0, 2)
    relay(1, 1)
    relay(0, 3)
    transform(0, 0, EARLY)
    relay(1, 2)
    relay(0, 4)
    transform(0, EARLY, PLANES)
    relay(1, 3)
    transform(1, 0, EARLY)
    relay(1, 4)
    transform(1, EARLY, PLANES)
    middle(0)
    middle(1)

    for h in range(2):
        part = restored.at[0, :, pl.ds(h * half, half)]
        pltpu.make_async_copy(part, part, back_recv.at[0, h]).wait()

        def one(k, _):
            partial[k] = backward(0, k)
            return 0

        lax.fori_loop(h * half, (h + 1) * half, one, 0)
    for h in range(2):
        part = restored.at[1, :, pl.ds(h * half, half)]
        pltpu.make_async_copy(part, part, back_recv.at[1, h]).wait()

        def one(k, _):
            p = plane(k)
            result[p] = -(partial[k] + backward(1, k))
            pltpu.make_async_copy(result.at[p], out_ref.at[0, p], out_sem.at[0]).start()
            return 0

        lax.fori_loop(h * half, (h + 1) * half, one, 0)

    part = gathered.at[pl.ds(0, 7)]
    pltpu.make_async_copy(part, part, spread_send.at[0]).wait()
    for o in range(2):
        part = held.at[o, pl.ds(0, 7)]
        pltpu.make_async_copy(part, part, tree_send.at[o]).wait()

        @pl.when(core == o)
        def _():
            part = ahead.at[o, pl.ds(0, CHIPS - 1)]
            pltpu.make_async_copy(part, part, ahead_send.at[o]).wait()

        @pl.when(core != o)
        def _():
            part = ahead.at[o]
            pltpu.make_async_copy(part, part, ahead_send.at[o]).wait()

    part = back.at[pl.ds(0, 31 * PLANES)]
    pltpu.make_async_copy(part, part, back_send.at[0]).wait()
    pltpu.make_async_copy(result, out_ref.at[0], out_sem.at[0]).wait()


def constants():
    positions = np.arange(POINTS)[:, None] * (np.arange(FREQS) - FREQS // 2)[None, :] % POINTS
    angles = positions * (2.0 * math.pi / POINTS)
    cas = np.cos(angles) + np.sin(angles)
    high = cas.astype(ml_dtypes.bfloat16)
    low = (cas - high.astype(np.float64)).astype(ml_dtypes.bfloat16)
    tall = np.concatenate([high, low], axis=1)
    wide = np.concatenate([high.T, low.T], axis=0)
    tall_x, wide_x = [], []
    for band in range(8):
        planes = [((band // 2 - r // 2) % 4) * 2 + (band + r) % 2 for r in ORDER]
        rows = np.concatenate([block * PLANES + np.array(planes) for block in range(POINTS // PLANES)])
        tall_x.append(tall[rows])
        wide_x.append(wide[:, rows])
    return tall, wide, np.stack(tall_x), np.stack(wide_x)


def exchange():
    dma = pltpu.SemaphoreType.DMA
    return pl.pallas_call(
        kernel,
        out_shape=jax.ShapeDtypeStruct((1, PLANES, POINTS, POINTS), F32),
        in_specs=[
            pl.BlockSpec(memory_space=pl.ANY),
            pl.BlockSpec(memory_space=pltpu.SMEM),
            pl.BlockSpec(memory_space=pltpu.SMEM),
            pl.BlockSpec(memory_space=pl.ANY),
            pl.BlockSpec(memory_space=pl.ANY),
            pl.BlockSpec(memory_space=pl.ANY),
            pl.BlockSpec(memory_space=pl.ANY),
        ],
        out_specs=pl.BlockSpec(memory_space=pl.ANY),
        scratch_shapes=[
            pltpu.VMEM((POINTS, 2 * FREQS), BF16),
            pltpu.VMEM((2 * FREQS, POINTS), BF16),
            pltpu.VMEM((POINTS, 2 * FREQS), BF16),
            pltpu.VMEM((2 * FREQS, POINTS), BF16),
            pltpu.VMEM((8, POINTS, POINTS), F32),
            pltpu.VMEM((2, PLANES, POINTS, POINTS), F32),
            pltpu.VMEM((PLANES, POINTS, POINTS), F32),
            pltpu.VMEM((2, CHIPS, PLANES, 8, FREQS), F32),
            pltpu.VMEM((POINTS, 8, FREQS), F32),
            pltpu.VMEM((POINTS, 8, FREQS), F32),
            pltpu.VMEM((2, CHIPS, PLANES, 8, FREQS), F32),
            pltpu.VMEM((8, FREQS, FREQS), F32),
            pltpu.VMEM((PLANES, POINTS, POINTS), F32),
            pltpu.VMEM((PLANES, POINTS, POINTS), F32),
            dma((5,)), dma((1,)), dma((1,)), dma((2,)), dma((2, 8, 3)),
            dma((2,)), dma((1,)), dma((1,)), dma((2, 2)), dma((1,)),
        ],
        compiler_params=pltpu.CompilerParams(
            collective_id=0, has_side_effects=True, vmem_limit_bytes=VMEM_MIB << 20
        ),
    )


def per_device(orbitals, band_ids, owners):
    tables = [jnp.asarray(c) for c in constants()]
    return exchange()(orbitals, band_ids, owners, *tables)


def solution(mesh):
    placed = (P("band", "fft", None, None), P(), P())
    return jax.shard_map(
        per_device,
        mesh=mesh,
        in_specs=placed,
        out_specs=P("band", "fft", None, None),
        check_vma=False,
    )
```

profile of v0, /device:TPU:1, one launch (start us, length us, event | category | flops | bytes accessed | tf_op | source)
XLA Modules:
  0.0 116.5 jit_solution(13376718434970499236)
XLA Ops:
  0.0 113.4 %shard_map.73 = f32[1,8,256,256]{3,2,1,0:T(8,128)} custom-call(f32[1,8,256,256]{3,2,1,0:T(8,128)} %orb_ref.1, s32[8]{0:T(128)} %ids_ref.1, s32[2]{0:T(128)} %owners_ref.1, bf16[256,256]{1,0:T(8,128)(2,1)} %constant.8.clone.tall_in, bf16[256,256]{1,0:T(8,128)(2,1)} %constant.9.clone.wide_in, bf16[8,256,256]{2,1,0:T(8,128)(2,1)} %constant.10.clone.tall_x_in, ...), custom_call_target="tpu_custom_call" | custom-call | tf_op jit(solution)/shard_map/pallas_call | solution.py:356
  113.4 3.0 %copy.9 = f32[1,8,256,256]{3,2,1,0:T(8,128)} copy(f32[1,8,256,256]{3,2,1,0:T(8,128)} %shard_map.73) | data formatting | bytes 4194304
where the time goes:
time: 117 us; the launch traced here: 116 us
  Pallas kernels  113 us (97%)
  local copies, waits for them, and re-layouts  3.05 us (3%)
    pallas_call x1, Pallas kernels, per_device(): return exchange()(orbitals, band_ids, owners, *tables)  113 us
    unnamed x1, local copies, waits for them, and re-layouts  3.05 us

commit v1 on v0

--- a/solution.py
+++ b/solution.py
@@ -1,3 +1,4 @@
+import itertools
 import math
 
 import jax
@@ -19,15 +20,35 @@
 PLANES = 8
 CHIPS = 16
 VMEM_MIB = 60
-ROWS = ((0, 88), (88, 88), (176, 80))
-ORDER = (0, 1, 2, 5, 6, 3, 4, 7)
-EARLY = 5
-TREES = (
+T_ROWS = ((0, 88), (88, 88), (176, 80))
+T_TREES = (
     ((0, 2, 4, 5), (3,), (2, 4)),
     ((7,), (0, 6, 4, 7, 5), (6,)),
     ((1, 3), (1,), (0, 3, 5, 7)),
 )
-DEPTHS = ((0, 3, 1, 2, 2, 3, 3, 4), (0, 3, 3, 4, 2, 3, 1, 2), (0, 1, 3, 2, 4, 3, 3, 2))
+T_DEPTHS = ((0, 3, 1, 2, 2, 3, 3, 4), (0, 3, 3, 4, 2, 3, 1, 2), (0, 1, 3, 2, 4, 3, 3, 2))
+T_ORDER = (0, 1, 2, 5, 6, 3, 4, 7)
+U_ROWS = ((0, 128), (128, 128))
+U_TREES = (((0, 2, 1, 3), (0, 1), (0,)), ((0, 1), (0, 6, 1, 7), (0,)))
+U_DEPTHS = ((0, 1, 1, 2, 2, 3, 1, 2), (0, 1, 1, 2, 2, 3, 1, 2))
+U_ORDER = (0, 1, 2, 6, 3, 7, 4, 5)
+T, U = (T_ROWS, T_TREES, T_DEPTHS, T_ORDER), (U_ROWS, U_TREES, U_DEPTHS, U_ORDER)
+SCHEMES = (T, T)
+PROGRAM = (
+    ("r", 0, 0), ("r", 1, 0), ("r", 0, 1), ("r", 0, 2), ("r", 1, 1), ("r", 0, 3), ("t", 0, 0, 5), ("r", 1, 2),
+    ("r", 0, 4), ("t", 0, 5, 8), ("r", 1, 3), ("t", 1, 0, 5), ("r", 1, 4), ("t", 1, 5, 8), ("m", 0), ("m", 1),
+)
+
+
+SENT = 7
+
+
+def ky_of(block, row):
+    plain = 6 * block + row - 48
+    plain = jnp.where(plain == -48, -64, plain)
+    inner = jnp.where(block < 8, 48 + block, -40 - block)
+    outer = jnp.where(block < 8, 63 - block, block - 71)
+    return jnp.where(row < 6, plain, jnp.where(row == 6, inner, outer))
 
 
 def split(value):
@@ -46,9 +67,9 @@
 
 
 def kernel(
-    orb_ref, ids_ref, owners_ref, tall_in, wide_in, tall_x_in, wide_x_in, out_ref,
-    tall_ref, wide_ref, tall_x, wide_x, gathered, held, own, ahead, arrived, back, restored, weights, partial, result,
-    in_sem, spread_send, spread_recv, tree_send, tree_recv, ahead_send, ahead_recv, back_send, back_recv, out_sem,
+    orb_ref, ids_ref, owners_ref, tall_in, wide_in, tall_y_in, wide_y_in, tall_x_in, wide_x_in, out_ref,
+    tall_ref, wide_ref, tall_y, wide_y, tall_x, wide_x, gathered, held, own, ahead, arrived, back, restored, weights, partial,
+    in_sem, met, spread_send, spread_recv, tree_send, tree_recv, ahead_send, ahead_recv, back_send, back_recv,
 ):
     band = lax.axis_index("band")
     place = lax.axis_index("fft")
@@ -61,6 +82,10 @@
     def source(relative):
         return band_at(4 - relative // 2, relative % 2)
 
+    def flipped(bit):
+        step = 1 << bit
+        return place + step - 2 * step * ((place // step) % 2)
+
     neighbours = (band_at(1, 0), band_at(3, 0), band_at(0, 1))
 
     load = pltpu.make_async_copy(orb_ref.at[0], own, in_sem.at[0])
@@ -68,8 +93,10 @@
     tables = (
         pltpu.make_async_copy(tall_in, tall_ref, in_sem.at[1]),
         pltpu.make_async_copy(wide_in, wide_ref, in_sem.at[2]),
-        pltpu.make_async_copy(tall_x_in.at[band], tall_x, in_sem.at[3]),
-        pltpu.make_async_copy(wide_x_in.at[band], wide_x, in_sem.at[4]),
+        pltpu.make_async_copy(tall_y_in, tall_y, in_sem.at[5]),
+        pltpu.make_async_copy(wide_y_in, wide_y, in_sem.at[6]),
+        pltpu.make_async_copy(tall_x_in.at[core, band], tall_x, in_sem.at[3]),
+        pltpu.make_async_copy(wide_x_in.at[core, band], wide_x, in_sem.at[4]),
     )
     for table in tables:
         table.start()
@@ -79,15 +106,11 @@
             barrier, inc=1, device_id=((band + k) % 8, place), device_id_type=MESH
         )
 
-    def greet(k, _):
+    for bit in range(5):
         pl.semaphore_signal(
-            barrier, inc=1, device_id=(band, (place + k) % 32), device_id_type=MESH
+            barrier, inc=1, device_id=(band, flipped(bit)), device_id_type=MESH
         )
-        return 0
-
-    lax.fori_loop(1, 32, greet, 0)
-
-    pl.semaphore_wait(barrier, 38)
+    pl.semaphore_wait(barrier, 12)
     for relative in (4, 5, 2, 6, 3, 7, 1):
         there = source(relative)
         pltpu.make_async_remote_copy(
@@ -99,16 +122,32 @@
     kx = lax.broadcasted_iota(jnp.int32, (FREQS, FREQS), 0) - FREQS // 2
     kz = lax.broadcasted_iota(jnp.int32, (FREQS, FREQS), 1) - FREQS // 2
 
+    turned = (kz + FREQS) % FREQS - FREQS // 2
+
     def weigh(row, _):
-        ky = chip * 8 + row - FREQS // 2
-        square = kx * kx + kz * kz + ky * ky
+        ky, ky_outer = ky_of(chip, row), ky_of(chip, 7)
+        outside = (row == 6) & (ky * ky + kz * kz >= FREQS * FREQS // 4)
+        square = jnp.where(
+            outside, ky_outer * ky_outer + turned * turned, ky * ky + kz * kz
+        ) + kx * kx
         inside = (square > 0) & (square < FREQS * FREQS // 4)
         safe = jnp.where(inside, square, 1).astype(F32)
         scale = cell_length**2 / math.pi / float(POINTS) ** 3
         weights[row] = jnp.where(inside, jnp.float32(scale) / safe, jnp.float32(0.0))
         return 0
 
-    lax.fori_loop(0, 8, weigh, 0)
+    row_in = (kx + FREQS // 2) % 8
+    ky = ky_of((kx + FREQS // 2) // 8, row_in)
+    in_disc = ky * ky + kz * kz < FREQS * FREQS // 4
+    take_outer = (row_in == 6) & jnp.logical_not(in_disc)
+
+    lax.fori_loop(0, SENT, weigh, 0)
+
+    for bit in range(5):
+        pl.semaphore_signal(
+            met.at[bit], inc=1, device_id=(band, flipped(bit)), device_id_type=MESH
+        )
+        pl.semaphore_wait(met.at[bit], 1)
 
     load.wait()
     for table in tables:
@@ -123,41 +162,44 @@
         held[o, band] = gathered[slot]
 
     def relay(o, depth):
-        for i, (first, count) in enumerate(ROWS):
+        table, trees, depths, _ = SCHEMES[o]
+        for i, (first, count) in enumerate(table):
             for relative in range(8):
-                if DEPTHS[i][relative] != depth:
+                if depths[i][relative] != depth:
                     continue
                 origin = source(relative)
                 part = held.at[o, origin, pl.ds(first, count)]
                 if depth:
                     pltpu.make_async_copy(part, part, tree_recv.at[o, origin, i]).wait()
                 for way in range(3):
-                    if relative in TREES[i][way]:
+                    if relative in trees[i][way]:
                         pltpu.make_async_remote_copy(
                             src_ref=part, dst_ref=part,
                             send_sem=tree_send.at[o], recv_sem=tree_recv.at[o, origin, i],
                             device_id=(neighbours[way], place), device_id_type=MESH,
                         ).start()
 
-    def plane(k):
-        return source(sum(jnp.where(k == n, relative, 0) for n, relative in enumerate(ORDER)))
+    def plane(o, k):
+        return source(sum(jnp.where(k == n, relative, 0) for n, relative in enumerate(SCHEMES[o][3])))
 
     def forward(o, k):
-        p = plane(k)
+        p = plane(o, k)
         density = held[o, p] * own[p]
         level = jnp.sum(density, keepdims=True) * (1.0 / POINTS**2)
         high, low = split(density - level)
         along_z = quarters(dot(jnp.concatenate([high, low], axis=0), tall_ref[...]))
         high, low = split(along_z)
-        along_y = quarters(dot(wide_ref[...], jnp.concatenate([high, low], axis=1)))
+        along_y = quarters(dot(wide_y[...], jnp.concatenate([high, low], axis=1)))
         along_y = along_y + jnp.where((kx == 0) & (kz == 0), level * float(POINTS**2), 0.0)
+        outer = pltpu.roll(pltpu.roll(along_y, FREQS - 1, 0), FREQS // 2, 1)
+        along_y = jnp.where(take_outer, outer, along_y)
         ahead[o, :, k] = along_y.reshape(CHIPS, 8, FREQS)
 
     def send_ahead(o, first, count):
         def one(k, _):
             there = (chip + k) % CHIPS
-            source = ahead.at[o, there, pl.ds(first, count)]
-            target = arrived.at[pl.ds(place * PLANES + first, count)]
+            source = ahead.at[o, there, pl.ds(first, count), pl.ds(0, SENT)]
+            target = arrived.at[pl.ds(place * PLANES + first, count), pl.ds(0, SENT)]
             here = there * 2 + o == place
 
             @pl.when(here)
@@ -189,7 +231,8 @@
     def middle(o):
         @pl.when(core == o)
         def _():
-            pltpu.make_async_copy(arrived, arrived, ahead_recv.at[0]).wait()
+            landed = arrived.at[:, pl.ds(0, SENT)]
+            pltpu.make_async_copy(landed, landed, ahead_recv.at[0]).wait()
 
             def one(row, _):
                 column = arrived[:, pl.ds(row, 1), :].reshape(POINTS, FREQS)
@@ -203,12 +246,12 @@
                 back[:, pl.ds(row, 1), :] = (both[:, :FREQS] + both[:, FREQS:]).reshape(POINTS, 1, FREQS)
                 return 0
 
-            lax.fori_loop(0, 8, one, 0, unroll=True)
+            lax.fori_loop(0, SENT, one, 0, unroll=True)
             for h in range(2):
                 def one(k, _):
                     there = (place + k) % 32
-                    source = back.at[pl.ds(there * PLANES + h * half, half)]
-                    target = restored.at[o, chip, pl.ds(h * half, half)]
+                    source = back.at[pl.ds(there * PLANES + h * half, half), pl.ds(0, SENT)]
+                    target = restored.at[o, chip, pl.ds(h * half, half), pl.ds(0, SENT)]
 
                     @pl.when(k == 0)
                     def _():
@@ -227,49 +270,36 @@
                 lax.fori_loop(0, 32, one, 0)
 
     def backward(o, k):
-        high, low = split(restored[o, :, k].reshape(FREQS, FREQS))
+        coeffs = restored[o, :, k].reshape(FREQS, FREQS)
+        outer = pltpu.roll(pltpu.roll(coeffs, 1, 0), FREQS // 2, 1)
+        coeffs = jnp.where(in_disc, jnp.where(row_in == 7, outer, coeffs), 0.0)
+        high, low = split(coeffs)
         pair = jnp.concatenate([high, low], axis=1)
-        both = dot(tall_ref[...], jnp.concatenate([pair, pair], axis=0))
+        both = dot(tall_y[...], jnp.concatenate([pair, pair], axis=0))
         high, low = split(both[:, :FREQS] + both[:, FREQS:])
         field = dot(jnp.concatenate([high, low], axis=1), jnp.concatenate([wide_ref[:FREQS], wide_ref[:FREQS]], axis=0))
         field = field + dot(high, wide_ref[FREQS:])
-        return held[o, plane(k)] * field
-        return held[o, plane(k)]
-
-    relay(0, 0)
-    relay(1, 0)
-    relay(0, 1)
-    relay(0, 2)
-    relay(1, 1)
-    relay(0, 3)
-    transform(0, 0, EARLY)
-    relay(1, 2)
-    relay(0, 4)
-    transform(0, EARLY, PLANES)
-    relay(1, 3)
-    transform(1, 0, EARLY)
-    relay(1, 4)
-    transform(1, EARLY, PLANES)
-    middle(0)
-    middle(1)
+        return held[o, plane(o, k)] * field
+
+    for name, *numbers in PROGRAM:
+        {"r": relay, "t": transform, "m": middle}[name](*numbers)
 
     for h in range(2):
-        part = restored.at[0, :, pl.ds(h * half, half)]
+        part = restored.at[0, :, pl.ds(h * half, half), pl.ds(0, SENT)]
         pltpu.make_async_copy(part, part, back_recv.at[0, h]).wait()
 
         def one(k, _):
-            partial[k] = backward(0, k)
+            partial[plane(0, k)] = backward(0, k)
             return 0
 
         lax.fori_loop(h * half, (h + 1) * half, one, 0)
     for h in range(2):
-        part = restored.at[1, :, pl.ds(h * half, half)]
+        part = restored.at[1, :, pl.ds(h * half, half), pl.ds(0, SENT)]
         pltpu.make_async_copy(part, part, back_recv.at[1, h]).wait()
 
         def one(k, _):
-            p = plane(k)
-            result[p] = -(partial[k] + backward(1, k))
-            pltpu.make_async_copy(result.at[p], out_ref.at[0, p], out_sem.at[0]).start()
+            p = plane(1, k)
+            out_ref[0, p] = -(partial[p] + backward(1, k))
             return 0
 
         lax.fori_loop(h * half, (h + 1) * half, one, 0)
@@ -282,34 +312,44 @@
 
         @pl.when(core == o)
         def _():
-            part = ahead.at[o, pl.ds(0, CHIPS - 1)]
+            part = ahead.at[o, pl.ds(0, CHIPS - 1), :, pl.ds(0, SENT)]
             pltpu.make_async_copy(part, part, ahead_send.at[o]).wait()
 
         @pl.when(core != o)
         def _():
-            part = ahead.at[o]
+            part = ahead.at[o, :, :, pl.ds(0, SENT)]
             pltpu.make_async_copy(part, part, ahead_send.at[o]).wait()
 
-    part = back.at[pl.ds(0, 31 * PLANES)]
+    part = back.at[pl.ds(0, 31 * PLANES), pl.ds(0, SENT)]
     pltpu.make_async_copy(part, part, back_send.at[0]).wait()
-    pltpu.make_async_copy(result, out_ref.at[0], out_sem.at[0]).wait()
-
-
-def constants():
-    positions = np.arange(POINTS)[:, None] * (np.arange(FREQS) - FREQS // 2)[None, :] % POINTS
+
+
+def cas_tables(freqs):
+    positions = np.arange(POINTS)[:, None] * freqs[None, :] % POINTS
     angles = positions * (2.0 * math.pi / POINTS)
     cas = np.cos(angles) + np.sin(angles)
     high = cas.astype(ml_dtypes.bfloat16)
     low = (cas - high.astype(np.float64)).astype(ml_dtypes.bfloat16)
     tall = np.concatenate([high, low], axis=1)
     wide = np.concatenate([high.T, low.T], axis=0)
+    return tall, wide
+
+
+def constants():
+    tall, wide = cas_tables(np.arange(FREQS) - FREQS // 2)
+    ky = []
+    for block in range(CHIPS):
+        ky += [6 * block + row - 48 for row in range(6)]
+        ky += [48 + block, 63 - block] if block < 8 else [-40 - block, block - 71]
+    ky[0] = -64
+    tall_y, wide_y = cas_tables(np.array(ky))
     tall_x, wide_x = [], []
-    for band in range(8):
-        planes = [((band // 2 - r // 2) % 4) * 2 + (band + r) % 2 for r in ORDER]
+    for o, band in itertools.product(range(2), range(8)):
+        planes = [((band // 2 - r // 2) % 4) * 2 + (band + r) % 2 for r in SCHEMES[o][3]]
         rows = np.concatenate([block * PLANES + np.array(planes) for block in range(POINTS // PLANES)])
         tall_x.append(tall[rows])
         wide_x.append(wide[:, rows])
-    return tall, wide, np.stack(tall_x), np.stack(wide_x)
+    return tall, wide, tall_y, wide_y, np.reshape(tall_x, (2, 8, *tall.shape)), np.reshape(wide_x, (2, 8, *wide.shape))
 
 
 def exchange():
@@ -325,9 +365,13 @@
             pl.BlockSpec(memory_space=pl.ANY),
             pl.BlockSpec(memory_space=pl.ANY),
             pl.BlockSpec(memory_space=pl.ANY),
+            pl.BlockSpec(memory_space=pl.ANY),
+            pl.BlockSpec(memory_space=pl.ANY),
         ],
-        out_specs=pl.BlockSpec(memory_space=pl.ANY),
+        out_specs=pl.BlockSpec(memory_space=pltpu.VMEM),
         scratch_shapes=[
+            pltpu.VMEM((POINTS, 2 * FREQS), BF16),
+            pltpu.VMEM((2 * FREQS, POINTS), BF16),
             pltpu.VMEM((POINTS, 2 * FREQS), BF16),
             pltpu.VMEM((2 * FREQS, POINTS), BF16),
             pltpu.VMEM((POINTS, 2 * FREQS), BF16),
@@ -341,9 +385,8 @@
             pltpu.VMEM((2, CHIPS, PLANES, 8, FREQS), F32),
             pltpu.VMEM((8, FREQS, FREQS), F32),
             pltpu.VMEM((PLANES, POINTS, POINTS), F32),
-            pltpu.VMEM((PLANES, POINTS, POINTS), F32),
-            dma((5,)), dma((1,)), dma((1,)), dma((2,)), dma((2, 8, 3)),
-            dma((2,)), dma((1,)), dma((1,)), dma((2, 2)), dma((1,)),
+            dma((7,)), pltpu.SemaphoreType.REGULAR((5,)), dma((1,)), dma((1,)), dma((2,)), dma((2, 8, 3)),
+            dma((2,)), dma((1,)), dma((1,)), dma((2, 2)),
         ],
         compiler_params=pltpu.CompilerParams(
             collective_id=0, has_side_effects=True, vmem_limit_bytes=VMEM_MIB << 20

time: 117 us -> 112 us (0.957)
  Pallas kernels: 113 us -> 109 us
    pallas_call x1, Pallas kernels: 113 us -> 109 us  [per_device(): return exchange()(orbitals, band_ids, owners, *tables)]
where the time goes in v1:
time: 112 us
  Pallas kernels  109 us (97%)
  local copies, waits for them, and re-layouts  3.05 us (3%)
    pallas_call x1, Pallas kernels, per_device(): return exchange()(orbitals, band_ids, owners, *tables)  109 us
    unnamed x1, local copies, waits for them, and re-layouts  3.05 us

profile of v1, /device:TPU:1, one launch (start us, length us, event | category | flops | bytes accessed | tf_op | source)
XLA Modules:
  0.0 112.2 jit_solution(14919234156255437032)
XLA Ops:
  0.0 109.2 %shard_map.91 = f32[1,8,256,256]{3,2,1,0:T(8,128)} custom-call(f32[1,8,256,256]{3,2,1,0:T(8,128)} %orb_ref.1, s32[8]{0:T(128)} %ids_ref.1, s32[2]{0:T(128)} %owners_ref.1, bf16[256,256]{1,0:T(8,128)(2,1)} %constant.12.clone.tall_in, bf16[256,256]{1,0:T(8,128)(2,1)} %constant.13.clone.wide_in, bf16[256,256]{1,0:T(8,128)(2,1)} %constant.14.clone.tall_y_in, ...), custom_call_target="tpu_custom_call" | custom-call | tf_op jit(solution)/shard_map/pallas_call | solution.py:399
  109.2 3.0 %copy.11 = f32[1,8,256,256]{3,2,1,0:T(8,128)} copy(f32[1,8,256,256]{3,2,1,0:T(8,128)} %shard_map.91) | data formatting | bytes 4194304

commit v2 on v1

--- a/solution.py
+++ b/solution.py
@@ -19,8 +19,7 @@
 FREQS = 128
 PLANES = 8
 CHIPS = 16
-VMEM_MIB = 60
-T_ROWS = ((0, 88), (88, 88), (176, 80))
+VMEM_MIB = 50
 T_TREES = (
     ((0, 2, 4, 5), (3,), (2, 4)),
     ((7,), (0, 6, 4, 7, 5), (6,)),
@@ -28,19 +27,18 @@
 )
 T_DEPTHS = ((0, 3, 1, 2, 2, 3, 3, 4), (0, 3, 3, 4, 2, 3, 1, 2), (0, 1, 3, 2, 4, 3, 3, 2))
 T_ORDER = (0, 1, 2, 5, 6, 3, 4, 7)
-U_ROWS = ((0, 128), (128, 128))
-U_TREES = (((0, 2, 1, 3), (0, 1), (0,)), ((0, 1), (0, 6, 1, 7), (0,)))
-U_DEPTHS = ((0, 1, 1, 2, 2, 3, 1, 2), (0, 1, 1, 2, 2, 3, 1, 2))
-U_ORDER = (0, 1, 2, 6, 3, 7, 4, 5)
-T, U = (T_ROWS, T_TREES, T_DEPTHS, T_ORDER), (U_ROWS, U_TREES, U_DEPTHS, U_ORDER)
-SCHEMES = (T, T)
+W = (((0, 48), (48, 40), (88, 40), (128, 40), (168, 48), (216, 40)), T_TREES * 2, T_DEPTHS * 2, T_ORDER)
+SCHEMES = (W, W)
 PROGRAM = (
     ("r", 0, 0), ("r", 1, 0), ("r", 0, 1), ("r", 0, 2), ("r", 1, 1), ("r", 0, 3), ("t", 0, 0, 5), ("r", 1, 2),
-    ("r", 0, 4), ("t", 0, 5, 8), ("r", 1, 3), ("t", 1, 0, 5), ("r", 1, 4), ("t", 1, 5, 8), ("m", 0), ("m", 1),
+    ("r", 0, 4), ("t", 0, 5, 8), ("r", 1, 3), ("t", 1, 0, 5), ("r", 1, 4), ("t", 1, 5, 8), ("m", 0),
+    ("b", 0, 0), ("b", 0, 1), ("m", 1), ("b", 1, 0), ("b", 1, 1), ("b", 1, 2), ("b", 1, 3),
 )
 
 
 SENT = 7
+UNROLL = True
+RETURNS = (2, 4)
 
 
 def ky_of(block, row):
@@ -67,9 +65,9 @@
 
 
 def kernel(
-    orb_ref, ids_ref, owners_ref, tall_in, wide_in, tall_y_in, wide_y_in, tall_x_in, wide_x_in, out_ref,
+    orb_ref, info_in, tables_in, out_ref,
     tall_ref, wide_ref, tall_y, wide_y, tall_x, wide_x, gathered, held, own, ahead, arrived, back, restored, weights, partial,
-    in_sem, met, spread_send, spread_recv, tree_send, tree_recv, ahead_send, ahead_recv, back_send, back_recv,
+    info_ref, in_sem, met, spread_send, spread_recv, tree_send, tree_recv, ahead_send, ahead_recv, back_send, back_recv,
 ):
     band = lax.axis_index("band")
     place = lax.axis_index("fft")
@@ -91,12 +89,13 @@
     load = pltpu.make_async_copy(orb_ref.at[0], own, in_sem.at[0])
     load.start()
     tables = (
-        pltpu.make_async_copy(tall_in, tall_ref, in_sem.at[1]),
-        pltpu.make_async_copy(wide_in, wide_ref, in_sem.at[2]),
-        pltpu.make_async_copy(tall_y_in, tall_y, in_sem.at[5]),
-        pltpu.make_async_copy(wide_y_in, wide_y, in_sem.at[6]),
-        pltpu.make_async_copy(tall_x_in.at[core, band], tall_x, in_sem.at[3]),
-        pltpu.make_async_copy(wide_x_in.at[core, band], wide_x, in_sem.at[4]),
+        pltpu.make_async_copy(info_in, info_ref, in_sem.at[7]),
+        pltpu.make_async_copy(tables_in.at[32], tall_ref, in_sem.at[1]),
+        pltpu.make_async_copy(tables_in.at[33], wide_ref, in_sem.at[2]),
+        pltpu.make_async_copy(tables_in.at[34], tall_y, in_sem.at[5]),
+        pltpu.make_async_copy(tables_in.at[35], wide_y, in_sem.at[6]),
+        pltpu.make_async_copy(tables_in.at[core * 8 + band], tall_x, in_sem.at[3]),
+        pltpu.make_async_copy(tables_in.at[core * 8 + band + 16], wide_x, in_sem.at[4]),
     )
     for table in tables:
         table.start()
@@ -158,7 +157,7 @@
     for o in range(2):
         slot = 0
         for s in range(1, 8):
-            slot = jnp.where(ids_ref[s] == owners_ref[o], s, slot)
+            slot = jnp.where(info_ref[s] == info_ref[8 + o], s, slot)
         held[o, band] = gathered[slot]
 
     def relay(o, depth):
@@ -196,27 +195,32 @@
         ahead[o, :, k] = along_y.reshape(CHIPS, 8, FREQS)
 
     def send_ahead(o, first, count):
+        def ends(there):
+            source = ahead.at[o, there, pl.ds(first, count), pl.ds(0, SENT)]
+            return source, arrived.at[pl.ds(place * PLANES + first, count), pl.ds(0, SENT)]
+
+        def send(there):
+            source, target = ends(there)
+            pltpu.make_async_remote_copy(
+                src_ref=source, dst_ref=target,
+                send_sem=ahead_send.at[o], recv_sem=ahead_recv.at[0],
+                device_id=(band, there * 2 + o), device_id_type=MESH,
+            ).start()
+
         def one(k, _):
-            there = (chip + k) % CHIPS
-            source = ahead.at[o, there, pl.ds(first, count), pl.ds(0, SENT)]
-            target = arrived.at[pl.ds(place * PLANES + first, count), pl.ds(0, SENT)]
-            here = there * 2 + o == place
-
-            @pl.when(here)
-            def _():
-                pltpu.make_async_copy(source, target, ahead_recv.at[0]).start()
-
-            @pl.when(jnp.logical_not(here))
-            def _():
-                pltpu.make_async_remote_copy(
-                    src_ref=source, dst_ref=target,
-                    send_sem=ahead_send.at[o], recv_sem=ahead_recv.at[0],
-                    device_id=(band, there * 2 + o), device_id_type=MESH,
-                ).start()
-
+            send((chip + k) % CHIPS)
             return 0
 
-        lax.fori_loop(0, CHIPS, one, 0)
+        @pl.when(core == o)
+        def _():
+            source, target = ends(chip)
+            pltpu.make_async_copy(source, target, ahead_recv.at[0]).start()
+
+        @pl.when(core != o)
+        def _():
+            send(chip)
+
+        lax.fori_loop(1, CHIPS, one, 0, unroll=UNROLL)
 
     def transform(o, first, last):
         def one(k, _):
@@ -226,7 +230,6 @@
         lax.fori_loop(first, last, one, 0)
         send_ahead(o, first, last - first)
 
-    half = PLANES // 2
 
     def middle(o):
         @pl.when(core == o)
@@ -247,27 +250,32 @@
                 return 0
 
             lax.fori_loop(0, SENT, one, 0, unroll=True)
-            for h in range(2):
-                def one(k, _):
-                    there = (place + k) % 32
-                    source = back.at[pl.ds(there * PLANES + h * half, half), pl.ds(0, SENT)]
-                    target = restored.at[o, chip, pl.ds(h * half, half), pl.ds(0, SENT)]
-
-                    @pl.when(k == 0)
-                    def _():
-                        pltpu.make_async_copy(source, target, back_recv.at[o, h]).start()
-
-                    @pl.when(k != 0)
-                    def _():
-                        pltpu.make_async_remote_copy(
-                            src_ref=source, dst_ref=target,
-                            send_sem=back_send.at[0], recv_sem=back_recv.at[o, h],
-                            device_id=(band, there), device_id_type=MESH,
-                        ).start()
-
-                    return 0
-
-                lax.fori_loop(0, 32, one, 0)
+    def group(o, h):
+        size = PLANES // RETURNS[o]
+        return h * size, size
+
+    def give_back(o, h):
+        first, size = group(o, h)
+
+        @pl.when(core == o)
+        def _():
+            def ends(there):
+                source = back.at[pl.ds(there * PLANES + first, size), pl.ds(0, SENT)]
+                return source, restored.at[o, chip, pl.ds(first, size), pl.ds(0, SENT)]
+
+            def one(k, _):
+                there = (place + k) % 32
+                source, target = ends(there)
+                pltpu.make_async_remote_copy(
+                    src_ref=source, dst_ref=target,
+                    send_sem=back_send.at[0], recv_sem=back_recv.at[o, h],
+                    device_id=(band, there), device_id_type=MESH,
+                ).start()
+                return 0
+
+            source, target = ends(place)
+            pltpu.make_async_copy(source, target, back_recv.at[o, h]).start()
+            lax.fori_loop(1, 32, one, 0, unroll=UNROLL)
 
     def backward(o, k):
         coeffs = restored[o, :, k].reshape(FREQS, FREQS)
@@ -282,19 +290,21 @@
         return held[o, plane(o, k)] * field
 
     for name, *numbers in PROGRAM:
-        {"r": relay, "t": transform, "m": middle}[name](*numbers)
-
-    for h in range(2):
-        part = restored.at[0, :, pl.ds(h * half, half), pl.ds(0, SENT)]
+        {"r": relay, "t": transform, "m": middle, "b": give_back}[name](*numbers)
+
+    for h in range(RETURNS[0]):
+        first, size = group(0, h)
+        part = restored.at[0, :, pl.ds(first, size), pl.ds(0, SENT)]
         pltpu.make_async_copy(part, part, back_recv.at[0, h]).wait()
 
         def one(k, _):
             partial[plane(0, k)] = backward(0, k)
             return 0
 
-        lax.fori_loop(h * half, (h + 1) * half, one, 0)
-    for h in range(2):
-        part = restored.at[1, :, pl.ds(h * half, half), pl.ds(0, SENT)]
+        lax.fori_loop(first, first + size, one, 0)
+    for h in range(RETURNS[1]):
+        first, size = group(1, h)
+        part = restored.at[1, :, pl.ds(first, size), pl.ds(0, SENT)]
         pltpu.make_async_copy(part, part, back_recv.at[1, h]).wait()
 
         def one(k, _):
@@ -302,7 +312,7 @@
             out_ref[0, p] = -(partial[p] + backward(1, k))
             return 0
 
-        lax.fori_loop(h * half, (h + 1) * half, one, 0)
+        lax.fori_loop(first, first + size, one, 0)
 
     part = gathered.at[pl.ds(0, 7)]
     pltpu.make_async_copy(part, part, spread_send.at[0]).wait()
@@ -349,7 +359,7 @@
         rows = np.concatenate([block * PLANES + np.array(planes) for block in range(POINTS // PLANES)])
         tall_x.append(tall[rows])
         wide_x.append(wide[:, rows])
-    return tall, wide, tall_y, wide_y, np.reshape(tall_x, (2, 8, *tall.shape)), np.reshape(wide_x, (2, 8, *wide.shape))
+    return np.stack(tall_x + wide_x + [tall, wide, tall_y, wide_y])
 
 
 def exchange():
@@ -357,17 +367,7 @@
     return pl.pallas_call(
         kernel,
         out_shape=jax.ShapeDtypeStruct((1, PLANES, POINTS, POINTS), F32),
-        in_specs=[
-            pl.BlockSpec(memory_space=pl.ANY),
-            pl.BlockSpec(memory_space=pltpu.SMEM),
-            pl.BlockSpec(memory_space=pltpu.SMEM),
-            pl.BlockSpec(memory_space=pl.ANY),
-            pl.BlockSpec(memory_space=pl.ANY),
-            pl.BlockSpec(memory_space=pl.ANY),
-            pl.BlockSpec(memory_space=pl.ANY),
-            pl.BlockSpec(memory_space=pl.ANY),
-            pl.BlockSpec(memory_space=pl.ANY),
-        ],
+        in_specs=[pl.BlockSpec(memory_space=pl.ANY)] * 3,
         out_specs=pl.BlockSpec(memory_space=pltpu.VMEM),
         scratch_shapes=[
             pltpu.VMEM((POINTS, 2 * FREQS), BF16),
@@ -385,8 +385,8 @@
             pltpu.VMEM((2, CHIPS, PLANES, 8, FREQS), F32),
             pltpu.VMEM((8, FREQS, FREQS), F32),
             pltpu.VMEM((PLANES, POINTS, POINTS), F32),
-            dma((7,)), pltpu.SemaphoreType.REGULAR((5,)), dma((1,)), dma((1,)), dma((2,)), dma((2, 8, 3)),
-            dma((2,)), dma((1,)), dma((1,)), dma((2, 2)),
+            pltpu.SMEM((10,), jnp.int32), dma((8,)), pltpu.SemaphoreType.REGULAR((5,)), dma((1,)), dma((1,)), dma((2,)), dma((2, 8, 6)),
+            dma((2,)), dma((1,)), dma((1,)), dma((2, max(RETURNS))),
         ],
         compiler_params=pltpu.CompilerParams(
             collective_id=0, has_side_effects=True, vmem_limit_bytes=VMEM_MIB << 20
@@ -395,8 +395,7 @@
 
 
 def per_device(orbitals, band_ids, owners):
-    tables = [jnp.asarray(c) for c in constants()]
-    return exchange()(orbitals, band_ids, owners, *tables)
+    return exchange()(orbitals, jnp.concatenate([band_ids, owners]), jnp.asarray(constants()))
 
 
 def solution(mesh):

time: 112 us -> 109 us (0.973)
  Pallas kernels: 109 us -> 106 us
  local copies, waits for them, and re-layouts: 3.05 us -> 1.32 us
    pallas_call x1, Pallas kernels: 109 us -> 106 us  [per_device(): exchange()]
    unnamed x1, local copies, waits for them, and re-layouts: 3.05 us -> 1.32 us
where the time goes in v2:
time: 109 us
  Pallas kernels  106 us (97%)
  local copies, waits for them, and re-layouts  1.32 us (1%)
    pallas_call x1, Pallas kernels, per_device(): exchange()  106 us

profile of v2, /device:TPU:1, one launch (start us, length us, event | category | flops | bytes accessed | tf_op | source)
XLA Modules:
  0.0 108.6 jit_solution(4727269415621367360)
XLA Ops:
  0.0 0.7 pad_add_fusion.info_in
  0.7 106.5 %shard_map.46 = f32[1,8,256,256]{3,2,1,0:T(8,128)S(1)} custom-call(f32[1,8,256,256]{3,2,1,0:T(8,128)} %orb_ref.1, s32[10]{0:T(128)S(1)} %pad_add_fusion.info_in, bf16[36,256,256]{2,1,0:T(8,128)(2,1)} %constant.2.clone.tables_in), custom_call_target="tpu_custom_call" | custom-call | tf_op jit(solution)/shard_map/pallas_call | solution.py:398
  107.2 1.3 %copy.6 = f32[1,8,256,256]{3,2,1,0:T(8,128)} copy(f32[1,8,256,256]{3,2,1,0:T(8,128)S(1)} %shard_map.46) | data formatting | bytes 4194304

commit v3 on v2

--- a/solution.py
+++ b/solution.py
@@ -30,9 +30,10 @@
 W = (((0, 48), (48, 40), (88, 40), (128, 40), (168, 48), (216, 40)), T_TREES * 2, T_DEPTHS * 2, T_ORDER)
 SCHEMES = (W, W)
 PROGRAM = (
-    ("r", 0, 0), ("r", 1, 0), ("r", 0, 1), ("r", 0, 2), ("r", 1, 1), ("r", 0, 3), ("t", 0, 0, 5), ("r", 1, 2),
-    ("r", 0, 4), ("t", 0, 5, 8), ("r", 1, 3), ("t", 1, 0, 5), ("r", 1, 4), ("t", 1, 5, 8), ("m", 0),
-    ("b", 0, 0), ("b", 0, 1), ("m", 1), ("b", 1, 0), ("b", 1, 1), ("b", 1, 2), ("b", 1, 3),
+    ("p", 0), ("r", 0, 0, 0), ("r", 1, 0, 0), ("p", 1), ("r", 0, 0, 1), ("r", 1, 0, 1), ("r", 0, 1),
+    ("r", 0, 2), ("r", 1, 1), ("r", 0, 3), ("t", 0, 0, 5), ("r", 1, 2), ("r", 0, 4), ("t", 0, 5, 8),
+    ("r", 1, 3), ("t", 1, 0, 5), ("r", 1, 4), ("t", 1, 5, 8), ("m", 0), ("b", 0, 0), ("b", 0, 1), ("m", 1),
+    ("b", 1, 0), ("b", 1, 1), ("b", 1, 2), ("b", 1, 3),
 )
 
 
@@ -66,7 +67,7 @@
 
 def kernel(
     orb_ref, info_in, tables_in, out_ref,
-    tall_ref, wide_ref, tall_y, wide_y, tall_x, wide_x, gathered, held, own, ahead, arrived, back, restored, weights, partial,
+    tall_ref, wide_ref, tall_y, wide_y, tall_x, wide_x, gathered_0, gathered_1, held, own, ahead, arrived, back, restored, weights, partial,
     info_ref, in_sem, met, spread_send, spread_recv, tree_send, tree_recv, ahead_send, ahead_recv, back_send, back_recv,
 ):
     band = lax.axis_index("band")
@@ -110,13 +111,17 @@
             barrier, inc=1, device_id=(band, flipped(bit)), device_id_type=MESH
         )
     pl.semaphore_wait(barrier, 12)
-    for relative in (4, 5, 2, 6, 3, 7, 1):
-        there = source(relative)
-        pltpu.make_async_remote_copy(
-            src_ref=orb_ref.at[0, there], dst_ref=gathered.at[band],
-            send_sem=spread_send.at[0], recv_sem=spread_recv.at[0],
-            device_id=(there, place), device_id_type=MESH,
-        ).start()
+    gathered = (gathered_0, gathered_1)
+    half_rows = POINTS // 2
+    for half in range(2):
+        rows = pl.ds(half * half_rows, half_rows)
+        for relative in (4, 5, 2, 6, 3, 7, 1):
+            there = source(relative)
+            pltpu.make_async_remote_copy(
+                src_ref=orb_ref.at[0, there, rows], dst_ref=gathered[half].at[band],
+                send_sem=spread_send.at[half], recv_sem=spread_recv.at[half],
+                device_id=(there, place), device_id_type=MESH,
+            ).start()
 
     kx = lax.broadcasted_iota(jnp.int32, (FREQS, FREQS), 0) - FREQS // 2
     kz = lax.broadcasted_iota(jnp.int32, (FREQS, FREQS), 1) - FREQS // 2
@@ -151,18 +156,26 @@
     load.wait()
     for table in tables:
         table.wait()
-    gathered[band] = own[band]
-    part = gathered.at[pl.ds(0, 7)]
-    pltpu.make_async_copy(part, part, spread_recv.at[0]).wait()
+    slots = []
     for o in range(2):
         slot = 0
         for s in range(1, 8):
             slot = jnp.where(info_ref[s] == info_ref[8 + o], s, slot)
-        held[o, band] = gathered[slot]
-
-    def relay(o, depth):
+        slots.append(slot)
+
+    def pick(half):
+        rows = pl.ds(half * half_rows, half_rows)
+        gathered[half][band] = own[band, rows]
+        part = gathered[half].at[pl.ds(0, 7)]
+        pltpu.make_async_copy(part, part, spread_recv.at[half]).wait()
+        for o in range(2):
+            held[o, band, rows] = gathered[half][slots[o]]
+
+    def relay(o, depth, *halves):
         table, trees, depths, _ = SCHEMES[o]
         for i, (first, count) in enumerate(table):
+            if halves and first // half_rows not in halves:
+                continue
             for relative in range(8):
                 if depths[i][relative] != depth:
                     continue
@@ -290,7 +303,7 @@
         return held[o, plane(o, k)] * field
 
     for name, *numbers in PROGRAM:
-        {"r": relay, "t": transform, "m": middle, "b": give_back}[name](*numbers)
+        {"r": relay, "p": pick, "t": transform, "m": middle, "b": give_back}[name](*numbers)
 
     for h in range(RETURNS[0]):
         first, size = group(0, h)
@@ -314,8 +327,9 @@
 
         lax.fori_loop(first, first + size, one, 0)
 
-    part = gathered.at[pl.ds(0, 7)]
-    pltpu.make_async_copy(part, part, spread_send.at[0]).wait()
+    for half in range(2):
+        part = gathered[half].at[pl.ds(0, 7)]
+        pltpu.make_async_copy(part, part, spread_send.at[half]).wait()
     for o in range(2):
         part = held.at[o, pl.ds(0, 7)]
         pltpu.make_async_copy(part, part, tree_send.at[o]).wait()
@@ -376,7 +390,8 @@
             pltpu.VMEM((2 * FREQS, POINTS), BF16),
             pltpu.VMEM((POINTS, 2 * FREQS), BF16),
             pltpu.VMEM((2 * FREQS, POINTS), BF16),
-            pltpu.VMEM((8, POINTS, POINTS), F32),
+            pltpu.VMEM((8, POINTS // 2, POINTS), F32),
+            pltpu.VMEM((8, POINTS // 2, POINTS), F32),
             pltpu.VMEM((2, PLANES, POINTS, POINTS), F32),
             pltpu.VMEM((PLANES, POINTS, POINTS), F32),
             pltpu.VMEM((2, CHIPS, PLANES, 8, FREQS), F32),
@@ -385,7 +400,7 @@
             pltpu.VMEM((2, CHIPS, PLANES, 8, FREQS), F32),
             pltpu.VMEM((8, FREQS, FREQS), F32),
             pltpu.VMEM((PLANES, POINTS, POINTS), F32),
-            pltpu.SMEM((10,), jnp.int32), dma((8,)), pltpu.SemaphoreType.REGULAR((5,)), dma((1,)), dma((1,)), dma((2,)), dma((2, 8, 6)),
+            pltpu.SMEM((10,), jnp.int32), dma((8,)), pltpu.SemaphoreType.REGULAR((5,)), dma((2,)), dma((2,)), dma((2,)), dma((2, 8, 6)),
             dma((2,)), dma((1,)), dma((1,)), dma((2, max(RETURNS))),
         ],
         compiler_params=pltpu.CompilerParams(

time: 109 us -> 104 us (0.954)
  Pallas kernels: 106 us -> 102 us
    pallas_call x1, Pallas kernels: 106 us -> 102 us  [per_device(): exchange()]
where the time goes in v3:
time: 104 us
  Pallas kernels  102 us (98%)
  local copies, waits for them, and re-layouts  1.32 us (1%)
    pallas_call x1, Pallas kernels, per_device(): exchange()  102 us

profile of v3, /device:TPU:1, one launch (start us, length us, event | category | flops | bytes accessed | tf_op | source)
XLA Modules:
  0.0 103.6 jit_solution(1514763707024060322)
XLA Ops:
  0.0 0.7 pad_add_fusion.info_in
  0.7 101.5 %shard_map.46 = f32[1,8,256,256]{3,2,1,0:T(8,128)S(1)} custom-call(f32[1,8,256,256]{3,2,1,0:T(8,128)} %orb_ref.1, s32[10]{0:T(128)S(1)} %pad_add_fusion.info_in, bf16[36,256,256]{2,1,0:T(8,128)(2,1)} %constant.2.clone.tables_in), custom_call_target="tpu_custom_call" | custom-call | tf_op jit(solution)/shard_map/pallas_call | solution.py:413
  102.3 1.3 %copy.6 = f32[1,8,256,256]{3,2,1,0:T(8,128)} copy(f32[1,8,256,256]{3,2,1,0:T(8,128)S(1)} %shard_map.46) | data formatting | bytes 4194304

commit v4 on v3

--- a/solution.py
+++ b/solution.py
@@ -30,10 +30,10 @@
 W = (((0, 48), (48, 40), (88, 40), (128, 40), (168, 48), (216, 40)), T_TREES * 2, T_DEPTHS * 2, T_ORDER)
 SCHEMES = (W, W)
 PROGRAM = (
-    ("p", 0), ("r", 0, 0, 0), ("r", 1, 0, 0), ("p", 1), ("r", 0, 0, 1), ("r", 1, 0, 1), ("r", 0, 1),
-    ("r", 0, 2), ("r", 1, 1), ("r", 0, 3), ("t", 0, 0, 5), ("r", 1, 2), ("r", 0, 4), ("t", 0, 5, 8),
-    ("r", 1, 3), ("t", 1, 0, 5), ("r", 1, 4), ("t", 1, 5, 8), ("m", 0), ("b", 0, 0), ("b", 0, 1), ("m", 1),
-    ("b", 1, 0), ("b", 1, 1), ("b", 1, 2), ("b", 1, 3),
+    ("p", 0), ("r", 0, 0, 0), ("r", 1, 0, 0), ("r", 0, 1, 0), ("p", 1), ("r", 0, 0, 1), ("r", 1, 0, 1),
+    ("r", 0, 1, 1), ("r", 0, 2), ("r", 1, 1), ("r", 0, 3), ("t", 0, 0, 5), ("r", 1, 2), ("r", 0, 4),
+    ("t", 0, 5, 8), ("r", 1, 3), ("t", 1, 0, 5), ("r", 1, 4), ("t", 1, 5, 8), ("m", 0), ("b", 0, 0),
+    ("b", 0, 1), ("m", 1), ("b", 1, 0), ("b", 1, 1), ("b", 1, 2), ("b", 1, 3),
 )
 
 
@@ -250,8 +250,8 @@
             landed = arrived.at[:, pl.ds(0, SENT)]
             pltpu.make_async_copy(landed, landed, ahead_recv.at[0]).wait()
 
-            def one(row, _):
-                column = arrived[:, pl.ds(row, 1), :].reshape(POINTS, FREQS)
+            for row in range(SENT):
+                column = arrived[:, row, :]
                 level = jnp.sum(column, axis=0, keepdims=True) * (1.0 / POINTS)
                 high, low = split(column - level)
                 along_x = quarters(dot(wide_x[...], jnp.concatenate([high, low], axis=1)))
@@ -259,10 +259,8 @@
                 high, low = split(along_x * weights[row])
                 pair = jnp.concatenate([high, low], axis=1)
                 both = dot(tall_x[...], jnp.concatenate([pair, pair], axis=0))
-                back[:, pl.ds(row, 1), :] = (both[:, :FREQS] + both[:, FREQS:]).reshape(POINTS, 1, FREQS)
-                return 0
-
-            lax.fori_loop(0, SENT, one, 0, unroll=True)
+                back[:, row, :] = both[:, :FREQS] + both[:, FREQS:]
+
     def group(o, h):
         size = PLANES // RETURNS[o]
         return h * size, size

time: 104 us -> 104 us (level)
  no operation moved by 1% of the time
where the time goes in v4:
time: 104 us
  Pallas kernels  102 us (98%)
  local copies, waits for them, and re-layouts  1.32 us (1%)
    pallas_call x1, Pallas kernels, per_device(): exchange()  102 us

profile of v4, /device:TPU:1, one launch (start us, length us, event | category | flops | bytes accessed | tf_op | source)
XLA Modules:
  0.0 103.8 jit_solution(4545823158520646824)
XLA Ops:
  0.0 0.7 pad_add_fusion.info_in
  0.7 101.8 %shard_map.46 = f32[1,8,256,256]{3,2,1,0:T(8,128)S(1)} custom-call(f32[1,8,256,256]{3,2,1,0:T(8,128)} %orb_ref.1, s32[10]{0:T(128)S(1)} %pad_add_fusion.info_in, bf16[36,256,256]{2,1,0:T(8,128)(2,1)} %constant.2.clone.tables_in), custom_call_target="tpu_custom_call" | custom-call | tf_op jit(solution)/shard_map/pallas_call | solution.py:411
  102.5 1.3 %copy.6 = f32[1,8,256,256]{3,2,1,0:T(8,128)} copy(f32[1,8,256,256]{3,2,1,0:T(8,128)S(1)} %shard_map.46) | data formatting | bytes 4194304
